TPU v7x, 32 devices: a whole 2x2x4 slice. The times are simulated.
32 devices in a mesh: col: 8 (over z, x), row: 4 (over y, core).
Axes of the slice: x: 2, y: 2, z: 4, core: 2. Of those that a mesh axis runs over, the one named last changes fastest.
Arguments:
- right_side: float32 [8, 256, 256], P('col'), may hold values from -6 to 6
- coupling: bfloat16 [2, 4, 256, 81920], P(None, 'row', None, 'col'), may hold values from -0.01953125 to 0.01953125
- child_solution: bfloat16 [81920, 256], P(('col', 'row')), may hold values from -6 to 6
- factor_blocks: bfloat16 [2, 4, 256, 8, 256], P(None, 'row', None, 'col'), may hold values from -1 to 1
- pattern: int32 [8, 8], replicated, may hold values from 0 to 1, as said below
- diag_inverse: bfloat16 [8, 256, 256], P('col'), may hold values from -0.375 to 0.375
Outputs:
- solved: bfloat16 [8, 256, 256], P('col')
Inputs may be any that keep to these rules, and one draw needn't show every extreme that they name: pattern[j, j - 1] = 1 for every j from 1 to 7; entries with k >= j are not read.
All inputs are finite; a program needn't handle non-finite values.
Results may differ from a plain program's by a relative error of at most 0.017.
Values may be sent and summed in bfloat16 or wider, within the bound.
A program may use at most 64 MiB of HBM per device.

v0:
```python
import jax
import jax.numpy as jnp
from jax import lax
from jax.sharding import PartitionSpec as P


def per_device(right_side, coupling, child_solution, factor_blocks, pattern, diag_inverse):
    nrow = lax.axis_size("row")
    ncol = lax.axis_size("col")
    row_index = lax.axis_index("row")
    col_index = lax.axis_index("col")
    brows = coupling.shape[0]
    blk_size = coupling.shape[2]
    kcols = coupling.shape[3]
    rhs_count = child_solution.shape[1]
    nblk = pattern.shape[0]
    group = ncol // nblk
    part_rows = blk_size // group
    my_block = col_index // group
    my_offset = col_index % group * part_rows
    flat = coupling.reshape(brows * blk_size, kcols)
    update = jnp.dot(
        flat,
        lax.all_gather(child_solution, "row", axis=0, tiled=True),
        preferred_element_type=jnp.float32,
    )
    update = update.reshape(brows, blk_size, rhs_count)
    rhs_part = right_side.reshape(part_rows, rhs_count)
    placed = lax.dynamic_update_slice(
        jnp.zeros((blk_size, rhs_count), jnp.float32), rhs_part, (my_offset, jnp.int32(0))
    )
    blocks = factor_blocks.reshape(brows, blk_size, part_rows)
    inv_rows = diag_inverse.reshape(part_rows, blk_size)

    def advance(j, solved):
        j_row = j % nrow
        j_arow = j // nrow
        flags = lax.dynamic_index_in_dim(pattern, j, 0, keepdims=False)
        flag = lax.dynamic_index_in_dim(flags, my_block, 0, keepdims=False)
        keep = (flag > 0) & (my_block < j)
        masked = jnp.where(keep, solved, jnp.zeros_like(solved))
        row_blocks = lax.dynamic_index_in_dim(blocks, j_arow, 0, keepdims=False)
        partial_value = jnp.dot(row_blocks, masked, preferred_element_type=jnp.float32)
        partial_value = partial_value + lax.dynamic_index_in_dim(update, j_arow, 0, keepdims=False)
        partial_value = jnp.where(my_block == j, placed, jnp.zeros_like(placed)) - partial_value
        partial_value = jnp.where(row_index == j_row, partial_value, jnp.zeros_like(partial_value))
        total = lax.psum(partial_value, ("col", "row"))
        fresh = jnp.dot(
            inv_rows, total.astype(jnp.bfloat16), preferred_element_type=jnp.float32
        ).astype(jnp.bfloat16)
        return jnp.where(my_block == j, fresh, solved)

    start_state = jnp.zeros((part_rows, rhs_count), jnp.bfloat16)
    solved = lax.fori_loop(0, nblk, advance, start_state)
    return solved.reshape(1, part_rows, rhs_count)


def solution(mesh):
    in_specs = (
        P("col", None, None),
        P(None, "row", None, "col"),
        P(("col", "row"), None),
        P(None, "row", None, "col", None),
        P(),
        P("col", None, None),
    )
    out_specs = P("col", None, None)
    return jax.shard_map(
        per_device, mesh=mesh, in_specs=in_specs, out_specs=out_specs, check_vma=False
    )
```

profile of v0, /device:TPU:25, one launch (start us, length us, event | category | flops | bytes accessed | tf_op | source)
XLA Modules:
  0.0 420.3 jit_solution(1928758109962869587)
XLA Ops:
  6.5 0.0 all-gather.2.cloned.1.call-start
  6.5 0.7 all-gather.2.cloned.1.call-update
  7.3 1.1 copy.7
  8.4 0.0 copy-start
  8.4 0.0 copy-start.1
  8.4 42.4 %all-gather.2.cloned.1.call-done = bf16[10240,256]{1,0:T(8,128)(2,1)} async-done(((bf16[2560,256]{1,0:T(8,128)(2,1)}), bf16[10240,256]{1,0:T(8,128)(2,1)}) %all-gather.2.cloned.1.call-update) | async-done | bytes 5242896 | tf_op jit(solution)/shard_map/all_gather | solution.py:24
  50.8 8.4 %fusion.12 = f32[2,256,256]{1,2,0:T(8,128)S(1)} fusion(bf16[2,1,256,10240]{3,2,1,0:T(8,128)(2,1)} %param.9, bf16[10240,256]{1,0:T(8,128)(2,1)} %all-gather.2.cloned.1.call-done), kind=kOutput, calls=%fused_computation.15 | convolution fusion | flops 2684354560 | bytes 16252928 | tf_op jit(solution)/shard_map/dot_general | solution.py:22
  59.2 0.0 copy-done
  59.2 0.0 copy-done.1
  59.2 353.5 %while.17 = (s32[]{:T(128)}, bf16[256,256]{0,1:T(8,128)(2,1)S(1)}, s32[]{:T(128)}, s32[]{:T(128)}, f32[256,256]{0,1:T(8,128)S(1)}, /*index=5*/bf16[2,256,256]{2,...) while((s32[]{:T(128)}, bf16[256,256]{0,1:T(8,128)(2,1)S(1)}, ...), condition=%wide.region_2.3_spmd.clone, body=%wide.region_0.2_spmd.clone.sunk | while | flops 67764248 | bytes 1969544 | solution.py:54
  59.2 1.3 dynamic_slice.47
  61.2 0.2 fusion.27
  61.4 39.7 %all-reduce.1 = bf16[256,256]{0,1:T(8,128)(2,1)S(1)} all-reduce(f32[256,256]{0,1:T(8,128)S(1)} %fusion.27), channel_id=1, replica_groups=mesh['col'=8,'row'=4] {'col','row'}, use_global_device_ids=true, to_apply=%region_1.1 | all-reduce | flops 65536 | bytes 393216 | tf_op jit(solution)/shard_map/while/body/eval_jaxpr/psum | solution.py:47
  101.1 0.2 fusion.28
  101.4 1.3 dynamic_slice.47
  103.3 0.2 fusion.27
  103.5 42.9 %all-reduce.1 = bf16[256,256]{0,1:T(8,128)(2,1)S(1)} all-reduce(f32[256,256]{0,1:T(8,128)S(1)} %fusion.27), channel_id=1, replica_groups=mesh['col'=8,'row'=4] {'col','row'}, use_global_device_ids=true, to_apply=%region_1.1 | all-reduce | flops 65536 | bytes 393216 | tf_op jit(solution)/shard_map/while/body/eval_jaxpr/psum | solution.py:47
  146.4 0.2 fusion.28
  146.7 1.3 dynamic_slice.47
  148.6 0.2 fusion.27
  148.9 40.8 %all-reduce.1 = bf16[256,256]{0,1:T(8,128)(2,1)S(1)} all-reduce(f32[256,256]{0,1:T(8,128)S(1)} %fusion.27), channel_id=1, replica_groups=mesh['col'=8,'row'=4] {'col','row'}, use_global_device_ids=true, to_apply=%region_1.1 | all-reduce | flops 65536 | bytes 393216 | tf_op jit(solution)/shard_map/while/body/eval_jaxpr/psum | solution.py:47
  189.7 0.2 fusion.28
  190.0 1.3 dynamic_slice.47
  191.9 0.2 fusion.27
  192.2 42.9 %all-reduce.1 = bf16[256,256]{0,1:T(8,128)(2,1)S(1)} all-reduce(f32[256,256]{0,1:T(8,128)S(1)} %fusion.27), channel_id=1, replica_groups=mesh['col'=8,'row'=4] {'col','row'}, use_global_device_ids=true, to_apply=%region_1.1 | all-reduce | flops 65536 | bytes 393216 | tf_op jit(solution)/shard_map/while/body/eval_jaxpr/psum | solution.py:47
  235.1 0.2 fusion.28
  235.4 1.3 dynamic_slice.47
  237.4 0.2 fusion.27
  237.6 40.7 %all-reduce.1 = bf16[256,256]{0,1:T(8,128)(2,1)S(1)} all-reduce(f32[256,256]{0,1:T(8,128)S(1)} %fusion.27), channel_id=1, replica_groups=mesh['col'=8,'row'=4] {'col','row'}, use_global_device_ids=true, to_apply=%region_1.1 | all-reduce | flops 65536 | bytes 393216 | tf_op jit(solution)/shard_map/while/body/eval_jaxpr/psum | solution.py:47
  278.3 0.2 fusion.28
  278.6 1.3 dynamic_slice.47
  280.6 0.2 fusion.27
  280.8 43.0 %all-reduce.1 = bf16[256,256]{0,1:T(8,128)(2,1)S(1)} all-reduce(f32[256,256]{0,1:T(8,128)S(1)} %fusion.27), channel_id=1, replica_groups=mesh['col'=8,'row'=4] {'col','row'}, use_global_device_ids=true, to_apply=%region_1.1 | all-reduce | flops 65536 | bytes 393216 | tf_op jit(solution)/shard_map/while/body/eval_jaxpr/psum | solution.py:47
  323.8 0.2 fusion.28
  324.1 1.3 dynamic_slice.47
  326.1 0.2 fusion.27
  326.3 40.7 %all-reduce.1 = bf16[256,256]{0,1:T(8,128)(2,1)S(1)} all-reduce(f32[256,256]{0,1:T(8,128)S(1)} %fusion.27), channel_id=1, replica_groups=mesh['col'=8,'row'=4] {'col','row'}, use_global_device_ids=true, to_apply=%region_1.1 | all-reduce | flops 65536 | bytes 393216 | tf_op jit(solution)/shard_map/while/body/eval_jaxpr/psum | solution.py:47
  367.0 0.2 fusion.28
  367.2 1.3 dynamic_slice.47
  369.2 0.2 fusion.27
  369.4 43.1 %all-reduce.1 = bf16[256,256]{0,1:T(8,128)(2,1)S(1)} all-reduce(f32[256,256]{0,1:T(8,128)S(1)} %fusion.27), channel_id=1, replica_groups=mesh['col'=8,'row'=4] {'col','row'}, use_global_device_ids=true, to_apply=%region_1.1 | all-reduce | flops 65536 | bytes 393216 | tf_op jit(solution)/shard_map/while/body/eval_jaxpr/psum | solution.py:47
  412.5 0.2 fusion.28
  412.7 0.8 copy.9
  (1 shorter events, 0.0 us)
Async XLA Ops:
  6.5 44.2 %all-gather.2.cloned.1.call-start = ((), (), s32[]{:S(2)}) async-start(), calls=%async_computation | async-start | bytes 6553600 | tf_op jit(solution)/shard_map/all_gather | solution.py:24
  8.4 50.8 %copy-start = (bf16[2,1,256,1,256]{4,2,3,1,0:T(8,128)(2,1)S(1)}, bf16[2,1,256,1,256]{4,2,3,1,0:T(8,128)(2,1)}, u32[]{:S(2)}) copy-start(bf16[2,1,256,1,256]{4,2,3,1,0:T(8,128)(2,1)} %param.11) | copy-start | bytes 786436
  8.4 50.8 %copy-start.1 = (bf16[1,256,256]{2,1,0:T(8,128)(2,1)S(1)}, bf16[1,256,256]{2,1,0:T(8,128)(2,1)}, u32[]{:S(2)}) copy-start(bf16[1,256,256]{2,1,0:T(8,128)(2,1)} %param.13) | copy-start | bytes 393220
Sparse Core Ops, SparseCore 0:
  8.9 41.8 all-gather.1
where the time goes:
time: 425 us; the launch traced here: 420 us
  blocking collectives  334 us (79%)
  waiting for transfers between devices  43.1 us (10%)
  between operations  13.5 us (3%)
  local copies, waits for them, and re-layouts  12.3 us (3%)
  matrix products  12.1 us (3%)
  loops' own time  5.51 us (1%)
    psum x8, blocking collectives, advance(): total = lax.psum(partial_value, ('col', 'row'))  334 us
    all_gather x1, waiting for transfers between devices, per_device(): lax.all_gather(child_solution, 'row', axis=0, tiled=True)  42.4 us
    dynamic_slice x8, local copies, waits for them, and re-layouts, advance(): flag = lax.dynamic_index_in_dim(flags, my_block, 0, keepdims=False)  10.5 us
  transfers between devices with their start and end apart: 1, of which 1 were waited for; matrix products, arithmetic and copies ran while one was open for 0% of the time, Pallas kernels for 0%

commit v1 on v0

--- a/solution.py
+++ b/solution.py
@@ -1,10 +1,303 @@
+import functools
+
 import jax
 import jax.numpy as jnp
 from jax import lax
+from jax.experimental import pallas as pl
+from jax.experimental.pallas import tpu as pltpu
 from jax.sharding import PartitionSpec as P
 
-
-def per_device(right_side, coupling, child_solution, factor_blocks, pattern, diag_inverse):
+MESH = pl.DeviceIdType.MESH
+BF16 = jnp.bfloat16
+F32 = jnp.float32
+
+
+def dot(a, b):
+    return jnp.dot(a, b, preferred_element_type=F32)
+
+
+def kernel(
+    nch, rhs_ref, cpl_hbm, child_hbm, fac_hbm, pat_ref, dinv_ref, out_ref,
+    cpl, gath, acc, fac, part, precv, diag, rside, rest, sol,
+    loc_sem, m_sem, y_send, y_recv, f_send, f_recv, fac_send, fac_recv,
+    d_sem, p_send, p_recv, ch_send, ch_recv, o_send, o_recv,
+):
+    nrow = lax.axis_size("row")
+    ncol = lax.axis_size("col")
+    nslab = ncol // 2
+    r = lax.axis_index("row")
+    c = lax.axis_index("col")
+    y, core = r // 2, r % 2
+    z, x = c // 2, c % 2
+    mate = 2 * y + 1 - core
+    across = 2 * (1 - y) + core
+    mate_across = 2 * (1 - y) + 1 - core
+    depth = child_hbm.shape[0]
+    step = depth // nch
+    half = rhs_ref.shape[2] // 2
+    solver = (core == 0) & (z % 2 == y)
+
+    def remote(src, dst, ss, rs, row, col):
+        return pltpu.make_async_remote_copy(
+            src_ref=src, dst_ref=dst, send_sem=ss, recv_sem=rs,
+            device_id={"row": row, "col": col}, device_id_type=MESH,
+        )
+
+    own = pltpu.make_async_copy(child_hbm, gath.at[r], loc_sem.at[0])
+    load = pltpu.make_async_copy(cpl_hbm, cpl, loc_sem.at[1])
+    own.start()
+    load.start()
+
+    barrier = pltpu.get_barrier_semaphore()
+    for dr in range(nrow):
+        for dc in range(ncol):
+            if dr or dc:
+                pl.semaphore_signal(
+                    barrier, inc=1,
+                    device_id={"row": (r + dr) % nrow, "col": (c + dc) % ncol},
+                    device_id_type=MESH,
+                )
+    pl.semaphore_wait(barrier, nrow * ncol - 1)
+
+    def rows(i):
+        return pl.ds(pl.multiple_of(i * step, step), step)
+
+    def y_copy(i):
+        return remote(child_hbm.at[rows(i)], gath.at[r, rows(i)], y_send.at[i], y_recv.at[i], across, c)
+
+    def y_arrival(i):
+        return remote(child_hbm.at[rows(i)], gath.at[across, rows(i)], y_send.at[i], y_recv.at[i], across, c)
+
+    def forward(i):
+        return remote(gath.at[across, rows(i)], gath.at[across, rows(i)], f_send.at[i], f_recv.at[i], mate, c)
+
+    def f_arrival(i):
+        return remote(
+            gath.at[mate_across, rows(i)], gath.at[mate_across, rows(i)], f_send.at[i], f_recv.at[i], mate, c)
+
+    for i in range(nch):
+        y_copy(i).start()
+    m_copy = remote(child_hbm, gath.at[r], m_sem.at[0], m_sem.at[1], mate, c)
+    m_copy.start()
+
+    def fac_copy(s, xd):
+        return remote(
+            fac_hbm.at[s], fac.at[core, c], fac_send.at[s, xd], fac_recv.at[core, c],
+            2 * y, 2 * (y + 2 * s) + xd)
+
+    for s in range(2):
+        @pl.when(c < r + nrow * s)
+        def _():
+            for xd in range(2):
+                fac_copy(s, xd).start()
+
+    d_copy = remote(dinv_ref.at[0], diag.at[x], d_sem.at[0], d_sem.at[1], r, c + 1 - 2 * x)
+    other_cols = pl.ds(pl.multiple_of((1 - x) * half, half), half)
+    my_cols = pl.ds(pl.multiple_of(x * half, half), half)
+    r_copy = remote(rhs_ref.at[0, :, other_cols], rside.at[x], d_sem.at[2], d_sem.at[3], r, c + 1 - 2 * x)
+
+    @pl.when(solver)
+    def _():
+        d_copy.start()
+        r_copy.start()
+        diag[x] = dinv_ref[0]
+        rside[x] = rhs_ref[0, :, my_cols]
+
+    acc[...] = jnp.zeros_like(acc)
+
+    def piece(slot, i):
+        cols = pl.ds(pl.multiple_of(slot * depth + i * step, step), step)
+        block = gath[slot, rows(i)]
+        for b in range(2):
+            acc[b] += dot(cpl[b, :, cols], block)
+
+    own.wait()
+    load.wait()
+
+    @pl.loop(0, nch)
+    def _(i):
+        piece(r, i)
+
+    remote(child_hbm, gath.at[mate], m_sem.at[0], m_sem.at[1], mate, c).wait_recv()
+
+    @pl.loop(0, nch)
+    def _(i):
+        piece(mate, i)
+
+    @pl.loop(0, nch)
+    def _(i):
+        y_arrival(i).wait_recv()
+        forward(i).start()
+        piece(across, i)
+        f_arrival(i).wait_recv()
+        piece(mate_across, i)
+
+    def p_copy(s, xd):
+        return remote(
+            part.at[s, xd], precv.at[core, c], p_send.at[s, xd], p_recv.at[core, c],
+            2 * y, 2 * (y + 2 * s) + xd)
+
+    def p_self(s, xd):
+        return solver & (c == 2 * (y + 2 * s) + xd)
+
+    for s in range(2):
+        for xd in range(2):
+            part[s, xd] = acc[s, :, xd * half:(xd + 1) * half].astype(BF16)
+
+            @pl.when(jnp.logical_not(p_self(s, xd)))
+            def _():
+                p_copy(s, xd).start()
+
+    def chain_copy(zd):
+        return remote(
+            sol.at[z], sol.at[z], ch_send.at[zd], ch_recv.at[z], 2 * (zd % 2), 2 * zd + x)
+
+    def out_copy(xo, ro):
+        return remote(
+            sol.at[z, xo], out_ref.at[0, :, my_cols], o_send.at[xo, ro], o_recv.at[x], ro, 2 * z + xo)
+
+    def out_self(xo, ro):
+        return (r == ro) & (x == xo)
+
+    @pl.when(solver)
+    def _():
+        mine = acc[z // 2, :, my_cols]
+        d_copy.wait_recv()
+        r_copy.wait_recv()
+        rest[0] = rside[0] - mine
+        rest[1] = rside[1]
+        for p in range(2):
+            for k in range(ncol):
+                slot = precv.at[p, k]
+
+                def take():
+                    remote(slot, slot, p_send.at[0, 0], p_recv.at[p, k], r, c).wait_recv()
+                    rest[p] = rest[p] - slot[...].astype(F32)
+
+                if p == 0:
+                    pl.when(c != k)(take)
+                else:
+                    take()
+        for p in range(2):
+            for k in range(ncol):
+                @pl.when(k < 2 * z + p)
+                def _():
+                    remote(
+                        fac.at[p, k], fac.at[p, k], fac_send.at[0, 0], fac_recv.at[p, k], r, c).wait_recv()
+
+        def term(p, k, value):
+            flag = jnp.where(pat_ref[2 * z + p, k] > 0, 1.0, 0.0).astype(F32)
+            rest[p] = rest[p] - flag * dot(fac[p, k], value)
+
+        for zz in range(nslab - 1):
+            @pl.when(zz < z)
+            def _():
+                remote(sol.at[zz], sol.at[zz], ch_send.at[0], ch_recv.at[zz], r, c).wait_recv()
+                for q in range(2):
+                    for p in range(2):
+                        term(p, 2 * zz + q, sol[zz, q])
+
+        first = dot(diag[0], rest[0].astype(BF16)).astype(BF16)
+        sol[z, 0] = first
+        term(1, 2 * z, first)
+        sol[z, 1] = dot(diag[1], rest[1].astype(BF16)).astype(BF16)
+        for zd in range(1, nslab):
+            @pl.when(zd > z)
+            def _():
+                chain_copy(zd).start()
+        for xo in range(2):
+            for ro in range(nrow):
+                @pl.when(jnp.logical_not(out_self(xo, ro)))
+                def _():
+                    out_copy(xo, ro).start()
+        out_ref[0, :, my_cols] = sol[z, x]
+
+    for xs in range(2):
+        @pl.when(jnp.logical_not(solver & (x == xs)))
+        def _():
+            spot = out_ref.at[0, :, pl.ds(xs * half, half)]
+            remote(sol.at[0, 0], spot, o_send.at[0, 0], o_recv.at[xs], r, c).wait_recv()
+
+    m_copy.wait_send()
+
+    @pl.loop(0, nch)
+    def _(i):
+        y_copy(i).wait_send()
+        forward(i).wait_send()
+
+    for s in range(2):
+        @pl.when(c < r + nrow * s)
+        def _():
+            for xd in range(2):
+                fac_copy(s, xd).wait_send()
+
+        for xd in range(2):
+            @pl.when(jnp.logical_not(p_self(s, xd)))
+            def _():
+                p_copy(s, xd).wait_send()
+
+    @pl.when(solver)
+    def _():
+        d_copy.wait_send()
+        r_copy.wait_send()
+        for zd in range(1, nslab):
+            @pl.when(zd > z)
+            def _():
+                chain_copy(zd).wait_send()
+        for xo in range(2):
+            for ro in range(nrow):
+                @pl.when(jnp.logical_not(out_self(xo, ro)))
+                def _():
+                    out_copy(xo, ro).wait_send()
+
+
+def fused(right_side, coupling, child_solution, factor_blocks, pattern, diag_inverse):
+    nrow = lax.axis_size("row")
+    ncol = lax.axis_size("col")
+    brows, _, bs, kcols = coupling.shape
+    depth, rhs = child_solution.shape
+    nch = depth // 256
+    half = rhs // 2
+    dma = pltpu.SemaphoreType.DMA
+    hbm = pl.BlockSpec(memory_space=pltpu.HBM)
+    vmem = pl.BlockSpec(memory_space=pltpu.VMEM)
+    flops = 2 * brows * bs * kcols * rhs
+    return pl.pallas_call(
+        functools.partial(kernel, nch),
+        out_shape=jax.ShapeDtypeStruct((1, bs, rhs), BF16),
+        in_specs=[vmem, hbm, hbm, hbm, pl.BlockSpec(memory_space=pltpu.SMEM), vmem],
+        out_specs=vmem,
+        scratch_shapes=[
+            pltpu.VMEM((brows, bs, kcols), BF16),
+            pltpu.VMEM((nrow, depth, rhs), BF16),
+            pltpu.VMEM((brows, bs, rhs), F32),
+            pltpu.VMEM((2, ncol, bs, bs), BF16),
+            pltpu.VMEM((2, 2, bs, half), BF16),
+            pltpu.VMEM((2, ncol, bs, half), BF16),
+            pltpu.VMEM((2, bs, bs), BF16),
+            pltpu.VMEM((2, bs, half), F32),
+            pltpu.VMEM((2, bs, half), F32),
+            pltpu.VMEM((ncol // 2, 2, bs, half), BF16),
+            dma((2,)), dma((2,)), dma((nch,)), dma((nch,)), dma((nch,)), dma((nch,)),
+            dma((2, 2)), dma((2, ncol)), dma((4,)), dma((2, 2)), dma((2, ncol)),
+            dma((ncol // 2,)), dma((ncol // 2,)), dma((2, nrow)), dma((2,)),
+        ],
+        compiler_params=pltpu.CompilerParams(
+            collective_id=0, has_side_effects=True, vmem_limit_bytes=48 * 1024 * 1024
+        ),
+        cost_estimate=pl.CostEstimate(
+            flops=flops, bytes_accessed=2 * brows * bs * kcols, transcendentals=0),
+    )(
+        right_side,
+        coupling.reshape(brows, bs, kcols),
+        child_solution,
+        factor_blocks.reshape(brows, bs, bs),
+        pattern,
+        diag_inverse,
+    )
+
+
+def general(right_side, coupling, child_solution, factor_blocks, pattern, diag_inverse):
     nrow = lax.axis_size("row")
     ncol = lax.axis_size("col")
     row_index = lax.axis_index("row")
@@ -56,6 +349,7 @@
 
 
 def solution(mesh):
+    nrow, ncol = mesh.shape["row"], mesh.shape["col"]
     in_specs = (
         P("col", None, None),
         P(None, "row", None, "col"),
@@ -64,7 +358,12 @@
         P(),
         P("col", None, None),
     )
-    out_specs = P("col", None, None)
+
+    def per_device(right_side, coupling, child_solution, factor_blocks, pattern, diag_inverse):
+        paired = nrow == 4 and ncol == 8 and pattern.shape[0] == 8
+        body = fused if paired else general
+        return body(right_side, coupling, child_solution, factor_blocks, pattern, diag_inverse)
+
     return jax.shard_map(
-        per_device, mesh=mesh, in_specs=in_specs, out_specs=out_specs, check_vma=False
-    )
+        per_device, mesh=mesh, in_specs=in_specs, out_specs=P("col", None, None), check_vma=False
+    )

time: 425 us -> 74 us (0.17)
  blocking collectives: 334 us -> 0 us
  Pallas kernels: 0 us -> 67.8 us
  waiting for transfers between devices: 43.1 us -> 0 us
  between operations: 13.5 us -> 0.01 us
  matrix products: 12.1 us -> 0 us
  local copies, waits for them, and re-layouts: 12.3 us -> 5.46 us
  loops' own time: 5.51 us -> 0 us
    psum x8 -> x0, blocking collectives: 334 us -> none  [advance(): total = lax.psum(partial_value, ('col', 'row'))]
    pallas_call x0 -> x1, Pallas kernels: none -> 67.8 us  [fused(): pl.pallas_call(functools.partial(kernel, nch), out_shape=jax.ShapeDtypeSt...]
    all_gather x1 -> x0, waiting for transfers between devices: 42.4 us -> none  [per_device(): lax.all_gather(child_solution, 'row', axis=0, tiled=True)]
    dot_general x17 -> x0, matrix products: 12.1 us -> none  [the longest x1 8.37 us: per_device(): jnp.dot(flat, lax.all_gather(child_solution, 'row', axis=0, tiled=True),...]
    dynamic_slice x8 -> x0, local copies, waits for them, and re-layouts: 10.5 us -> none  [advance(): flag = lax.dynamic_index_in_dim(flags, my_block, 0, keepdims=False)]
    another operation x1 -> x0, loops' own time: 5.51 us -> none  [per_device(): solved = lax.fori_loop(0, nblk, advance, start_state)]
    unnamed x5 -> x11, local copies, waits for them, and re-layouts: 1.09 us -> 5.46 us
  transfers between devices with their start and end apart: 1 -> 0, of which waited for: 1 -> 0; matrix products, arithmetic and copies ran while one was open for 0% -> 0% of each run, Pallas kernels for 0% -> 0%
where the time goes in v1:
time: 74 us; the launch traced here: 73.3 us
  Pallas kernels  67.8 us (92%)
  local copies, waits for them, and re-layouts  5.46 us (7%)
    pallas_call x1, Pallas kernels, fused(): pl.pallas_call(functools.partial(kernel, nch), out_shape=jax.ShapeDtypeSt...  67.8 us
    unnamed x11, local copies, waits for them, and re-layouts  5.46 us

profile of v1, /device:TPU:25, one launch (start us, length us, event | category | flops | bytes accessed | tf_op | source)
XLA Modules:
  0.0 73.3 jit_solution(1632883866970245761)
XLA Ops:
  0.0 0.0 copy-start
  0.0 1.3 %copy-done = bf16[2560,256]{1,0:T(8,128)(2,1)S(1)} copy-done((bf16[2560,256]{1,0:T(8,128)(2,1)S(1)}, bf16[2560,256]{1,0:T(8,128)(2,1)}, u32[]{:S(2)}) %copy-start) | copy-done | bytes 1310744
  1.3 0.0 copy-start.1
  1.3 0.9 %copy-done.1 = f32[1,256,256]{2,1,0:T(8,128)S(1)} copy-done((f32[1,256,256]{2,1,0:T(8,128)S(1)}, f32[1,256,256]{2,1,0:T(8,128)}, u32[]{:S(2)}) %copy-start.1) | copy-done | bytes 262168
  2.3 0.0 copy-start.2
  2.3 0.9 %copy-done.2 = bf16[2,1,256,1,256]{4,2,3,1,0:T(8,128)(2,1)S(1)} copy-done((bf16[2,1,256,1,256]{4,2,3,1,0:T(8,128)(2,1)S(1)}, bf16[2,1,256,1,256]{4,2,3,1,0:T(8,128)(2,1)}, u32[]{:S(2)}) %copy-start.2) | copy-done | bytes 262168
  3.2 0.0 copy-start.3
  3.2 0.9 %copy-done.3 = bf16[1,256,256]{2,1,0:T(8,128)(2,1)S(1)} copy-done((bf16[1,256,256]{2,1,0:T(8,128)(2,1)S(1)}, bf16[1,256,256]{2,1,0:T(8,128)(2,1)}, u32[]{:S(2)}) %copy-start.3) | copy-done | bytes 131096
  4.1 0.0 copy-start.4
  4.1 0.7 copy-done.4
  4.8 67.8 %shard_map.64 = bf16[1,256,256]{2,1,0:T(8,128)(2,1)S(1)} custom-call(f32[1,256,256]{2,1,0:T(8,128)S(1)} %copy-done.1, bf16[2,256,10240]{2,1,0:T(8,128)(2,1)} %bitcast.3, bf16[2560,256]{1,0:T(8,128)(2,1)S(1)} %copy-done, bf16[2,256,256]{2,1,0:T(8,128)(2,1)S(1)} %bitcast.2, s32[8,8]{1,0:T(8,128)S(1)} %copy-done.4, bf16[1,256,256]{2,1,0:T(8,128)(2,1)S(1)} %copy-done.3), custom_call_target="tpu_custom_call" | custom-call | flops 2684354560 | bytes 10485760 | tf_op jit(solution)/shard_map/pallas_call | solution.py:265
  72.7 0.7 copy.8
Async XLA Ops:
  0.0 1.3 %copy-start = (bf16[2560,256]{1,0:T(8,128)(2,1)S(1)}, bf16[2560,256]{1,0:T(8,128)(2,1)}, u32[]{:S(2)}) copy-start(bf16[2560,256]{1,0:T(8,128)(2,1)} %child_hbm.1) | copy-start | bytes 3932164
  1.3 0.9 %copy-start.1 = (f32[1,256,256]{2,1,0:T(8,128)S(1)}, f32[1,256,256]{2,1,0:T(8,128)}, u32[]{:S(2)}) copy-start(f32[1,256,256]{2,1,0:T(8,128)} %rhs_ref.1) | copy-start | bytes 786436
  2.3 0.9 %copy-start.2 = (bf16[2,1,256,1,256]{4,2,3,1,0:T(8,128)(2,1)S(1)}, bf16[2,1,256,1,256]{4,2,3,1,0:T(8,128)(2,1)}, u32[]{:S(2)}) copy-start(bf16[2,1,256,1,256]{4,2,3,1,0:T(8,128)(2,1)} %param.9) | copy-start | bytes 786436
  3.2 0.9 %copy-start.3 = (bf16[1,256,256]{2,1,0:T(8,128)(2,1)S(1)}, bf16[1,256,256]{2,1,0:T(8,128)(2,1)}, u32[]{:S(2)}) copy-start(bf16[1,256,256]{2,1,0:T(8,128)(2,1)} %dinv_ref.1) | copy-start | bytes 393220
  4.1 0.7 copy-start.4

commit v2 on v1

v2 whole, which is shorter than its diff:
```python
import functools

import jax
import jax.numpy as jnp
from jax import lax
from jax.experimental import pallas as pl
from jax.experimental.pallas import tpu as pltpu
from jax.sharding import PartitionSpec as P

MESH = pl.DeviceIdType.MESH
BF16 = jnp.bfloat16
F32 = jnp.float32


def dot(a, b):
    return jnp.dot(a, b, preferred_element_type=F32)


def kernel(
    nch, rhs_hbm, cpl_hbm, child_hbm, fac_hbm, pat_hbm, dinv_hbm, out_ref,
    pat_ref, cpl, gath, acc, fac, xpart, xrecv, part, precv, diag, rside, below, gain, rest, sol,
    loc_sem, m_send, m_recv, y_send, y_recv, f_send, f_recv, fac_send, fac_recv,
    d_sem, x_sem, p_send, p_recv, ch_send, ch_recv, o_send, o_recv,
):
    nrow = lax.axis_size("row")
    ncol = lax.axis_size("col")
    nslab = ncol // 2
    r = lax.axis_index("row")
    c = lax.axis_index("col")
    y, core = r // 2, r % 2
    z, x = c // 2, c % 2
    mate = 2 * y + 1 - core
    across = 2 * (1 - y) + core
    mate_across = 2 * (1 - y) + 1 - core
    beside = c + 1 - 2 * x
    depth = child_hbm.shape[0]
    step = depth // nch
    half = rhs_hbm.shape[2] // 2
    solver = (core == 0) & (z % 2 == y)
    other_cols = pl.ds(pl.multiple_of((1 - x) * half, half), half)
    my_cols = pl.ds(pl.multiple_of(x * half, half), half)
    halves = (other_cols, my_cols)

    def remote(src, dst, ss, rs, row, col):
        return pltpu.make_async_remote_copy(
            src_ref=src, dst_ref=dst, send_sem=ss, recv_sem=rs,
            device_id={"row": row, "col": col}, device_id_type=MESH,
        )

    def arrival(ref, sem):
        return remote(ref, ref, d_sem.at[0], sem, mate, c)

    own = [
        pltpu.make_async_copy(child_hbm.at[:, halves[h]], gath.at[h, r], loc_sem.at[h])
        for h in range(2)
    ]
    load = pltpu.make_async_copy(cpl_hbm, cpl, loc_sem.at[2])
    flags = pltpu.make_async_copy(pat_hbm, pat_ref, loc_sem.at[3])
    d_own = pltpu.make_async_copy(dinv_hbm.at[0], diag.at[x], loc_sem.at[4])
    r_own = pltpu.make_async_copy(rhs_hbm.at[0, :, my_cols], rside.at[x], loc_sem.at[5])
    for copy in (own[0], own[1], load, flags, d_own, r_own):
        copy.start()

    barrier = pltpu.get_barrier_semaphore()
    for dr in range(nrow):
        for dc in range(ncol):
            if dr or dc:
                pl.semaphore_signal(
                    barrier, inc=1,
                    device_id={"row": (r + dr) % nrow, "col": (c + dc) % ncol},
                    device_id_type=MESH,
                )
    pl.semaphore_wait(barrier, nrow * ncol - 1)

    def rows(i):
        return pl.ds(pl.multiple_of(i * step, step), step)

    def y_copy(h, i):
        return remote(
            child_hbm.at[rows(i), halves[h]], gath.at[h, r, rows(i)],
            y_send.at[h, i], y_recv.at[h, i], across, c)

    def forward(h, i):
        spot = gath.at[h, across, rows(i)]
        return remote(spot, spot, f_send.at[h, i], f_recv.at[h, i], mate, c)

    def m_copy(h):
        return remote(
            child_hbm.at[:, halves[h]], gath.at[h, r], m_send.at[h], m_recv.at[h], mate, c)

    for i in range(nch):
        y_copy(0, i).start()
    for h in range(2):
        m_copy(h).start()

    def fac_copy(s, xd):
        return remote(
            fac_hbm.at[s], fac.at[core, c], fac_send.at[s, xd], fac_recv.at[core, c],
            2 * y, 2 * (y + 2 * s) + xd)

    for s in range(2):
        @pl.when(c < r + nrow * s)
        def _():
            for xd in range(2):
                fac_copy(s, xd).start()

    d_copy = remote(dinv_hbm.at[0], diag.at[x], d_sem.at[0], d_sem.at[1], r, beside)
    r_copy = remote(rhs_hbm.at[0, :, other_cols], rside.at[x], d_sem.at[2], d_sem.at[3], r, beside)

    @pl.when(solver)
    def _():
        d_copy.start()
        r_copy.start()

    acc[...] = jnp.zeros_like(acc)

    def piece(h, slot, i):
        cols = pl.ds(pl.multiple_of(slot * depth + i * step, step), step)
        block = gath[h, slot, rows(i)]
        for b in range(2):
            acc[h, b] += dot(cpl[b, :, cols], block)

    def flag(p, k):
        return jnp.where(pat_ref[2 * z + p, k] > 0, 1.0, 0.0).astype(F32)

    def prepare():
        d_own.wait()
        r_own.wait()
        arrival(diag.at[1 - x], d_sem.at[1]).wait_recv()
        arrival(rside.at[1 - x], d_sem.at[3]).wait_recv()
        for p in range(2):
            for k in range(ncol - 1):
                @pl.when(k < 2 * z + p)
                def _():
                    arrival(fac.at[p, k], fac_recv.at[p, k]).wait_recv()
        inner = flag(1, 2 * z) * dot(fac[1, 2 * z], diag[0])
        below[...] = -dot(diag[1], inner.astype(BF16)).astype(BF16)
        for zz in range(nslab - 1):
            @pl.when(zz < z)
            def _():
                @pl.loop(0, 2)
                def _(q):
                    k = 2 * zz + q
                    gain[zz, q, 0] = (flag(0, k) * dot(diag[0], fac[0, k])).astype(BF16)
                    gain[zz, q, 1] = (
                        flag(1, k) * dot(diag[1], fac[1, k]) + flag(0, k) * dot(below[...], fac[0, k])
                    ).astype(BF16)

    flags.wait()
    load.wait()
    for h in range(2):
        own[h].wait()

        @pl.loop(0, nch)
        def _(i):
            piece(h, r, i)

        arrival(gath.at[h, mate], m_recv.at[h]).wait_recv()

        @pl.loop(0, nch)
        def _(i):
            piece(h, mate, i)

        if h == 1:
            continue

        @pl.loop(0, nch)
        def _(i):
            arrival(gath.at[0, across, rows(i)], y_recv.at[0, i]).wait_recv()
            y_copy(1, i).start()
            forward(0, i).start()
            piece(0, across, i)
            arrival(gath.at[0, mate_across, rows(i)], f_recv.at[0, i]).wait_recv()
            piece(0, mate_across, i)

        xpart[...] = acc[0].astype(BF16)
        x_copy = remote(xpart, xrecv, x_sem.at[0], x_sem.at[1], r, beside)
        x_copy.start()
        pl.when(solver)(prepare)

    @pl.loop(0, nch)
    def _(i):
        arrival(gath.at[1, across, rows(i)], y_recv.at[1, i]).wait_recv()
        forward(1, i).start()
        piece(1, across, i)
        arrival(gath.at[1, mate_across, rows(i)], f_recv.at[1, i]).wait_recv()
        piece(1, mate_across, i)

    x_copy.wait_recv()

    def p_copy(s):
        return remote(
            part.at[s], precv.at[core, z], p_send.at[s], p_recv.at[core, z],
            2 * y, 2 * (y + 2 * s) + x)

    def p_self(s):
        return solver & (z == y + 2 * s)

    for s in range(2):
        acc[1, s] = acc[1, s] + xrecv[s].astype(F32)
        part[s] = acc[1, s].astype(BF16)

        @pl.when(jnp.logical_not(p_self(s)))
        def _():
            p_copy(s).start()

    def chain_copy(zd):
        return remote(
            sol.at[z], sol.at[z], ch_send.at[zd], ch_recv.at[z], 2 * (zd % 2), 2 * zd + x)

    def out_copy(xo, ro):
        return remote(
            sol.at[z, xo], out_ref.at[0, :, my_cols], o_send.at[xo, ro], o_recv.at[x], ro, 2 * z + xo)

    def out_self(xo, ro):
        return (r == ro) & (x == xo)

    def send_out(xo):
        for ro in range(nrow):
            @pl.when(jnp.logical_not(out_self(xo, ro)))
            def _():
                out_copy(xo, ro).start()

    @pl.when(jnp.logical_not(solver))
    def _():
        d_own.wait()
        r_own.wait()

    @pl.when(solver)
    def _():
        rest[0] = rside[0] - acc[1, z // 2]
        rest[1] = rside[1]
        for p in range(2):
            for k in range(nslab):
                def take():
                    arrival(precv.at[p, k], p_recv.at[p, k]).wait_recv()
                    rest[p] = rest[p] - precv[p, k].astype(F32)

                if p == 0:
                    pl.when(z != k)(take)
                else:
                    take()

        upper = rest[0].astype(BF16)
        lower = rest[1].astype(BF16)
        rest[0] = dot(diag[0], upper)
        rest[1] = dot(diag[1], lower) + dot(below[...], upper)
        for zz in range(nslab - 1):
            @pl.when(zz < z)
            def _():
                arrival(sol.at[zz], ch_recv.at[zz]).wait_recv()
                for p in range(2):
                    rest[p] = rest[p] - (dot(gain[zz, 0, p], sol[zz, 0]) + dot(gain[zz, 1, p], sol[zz, 1]))

        sol[z] = rest[...].astype(BF16)
        for zd in range(1, nslab):
            @pl.when(zd == z + 1)
            def _():
                chain_copy(zd).start()
                chain_copy(zd).wait_send()
        for zd in range(2, nslab):
            @pl.when(zd > z + 1)
            def _():
                chain_copy(zd).start()
        send_out(0)
        send_out(1)
        out_ref[0, :, my_cols] = sol[z, x]

    m_copy(0).wait_send()
    m_copy(1).wait_send()
    x_copy.wait_send()
    for h in range(2):
        @pl.loop(0, nch)
        def _(i):
            y_copy(h, i).wait_send()
            forward(h, i).wait_send()

    for s in range(2):
        @pl.when(c < r + nrow * s)
        def _():
            for xd in range(2):
                fac_copy(s, xd).wait_send()

        @pl.when(jnp.logical_not(p_self(s)))
        def _():
            p_copy(s).wait_send()

    for xs in range(2):
        @pl.when(jnp.logical_not(solver & (x == xs)))
        def _():
            arrival(out_ref.at[0, :, pl.ds(xs * half, half)], o_recv.at[xs]).wait_recv()

    @pl.when(solver)
    def _():
        d_copy.wait_send()
        r_copy.wait_send()
        for zd in range(2, nslab):
            @pl.when(zd > z + 1)
            def _():
                chain_copy(zd).wait_send()
        for xo in range(2):
            for ro in range(nrow):
                @pl.when(jnp.logical_not(out_self(xo, ro)))
                def _():
                    out_copy(xo, ro).wait_send()


def fused(right_side, coupling, child_solution, factor_blocks, pattern, diag_inverse):
    nrow = lax.axis_size("row")
    ncol = lax.axis_size("col")
    brows, _, bs, kcols = coupling.shape
    depth, rhs = child_solution.shape
    nch = depth // 512
    half = rhs // 2
    dma = pltpu.SemaphoreType.DMA
    hbm = pl.BlockSpec(memory_space=pltpu.HBM)
    vmem = pl.BlockSpec(memory_space=pltpu.VMEM)
    flops = 2 * brows * bs * kcols * rhs
    return pl.pallas_call(
        functools.partial(kernel, nch),
        out_shape=jax.ShapeDtypeStruct((1, bs, rhs), BF16),
        in_specs=[hbm] * 6,
        out_specs=vmem,
        scratch_shapes=[
            pltpu.SMEM(pattern.shape, pattern.dtype),
            pltpu.VMEM((brows, bs, kcols), BF16),
            pltpu.VMEM((2, nrow, depth, half), BF16),
            pltpu.VMEM((2, brows, bs, half), F32),
            pltpu.VMEM((2, ncol, bs, bs), BF16),
            pltpu.VMEM((brows, bs, half), BF16),
            pltpu.VMEM((brows, bs, half), BF16),
            pltpu.VMEM((brows, bs, half), BF16),
            pltpu.VMEM((2, ncol // 2, bs, half), BF16),
            pltpu.VMEM((2, bs, bs), BF16),
            pltpu.VMEM((2, bs, half), F32),
            pltpu.VMEM((bs, bs), BF16),
            pltpu.VMEM((ncol // 2 - 1, 2, 2, bs, bs), BF16),
            pltpu.VMEM((2, bs, half), F32),
            pltpu.VMEM((ncol // 2, 2, bs, half), BF16),
            dma((6,)), dma((2,)), dma((2,)),
            dma((2, nch)), dma((2, nch)), dma((2, nch)), dma((2, nch)),
            dma((2, 2)), dma((2, ncol)), dma((4,)), dma((2,)), dma((2,)), dma((2, ncol // 2)),
            dma((ncol // 2,)), dma((ncol // 2,)), dma((2, nrow)), dma((2,)),
        ],
        compiler_params=pltpu.CompilerParams(
            collective_id=0, has_side_effects=True, vmem_limit_bytes=62 * 1024 * 1024
        ),
        cost_estimate=pl.CostEstimate(
            flops=flops, bytes_accessed=2 * brows * bs * kcols, transcendentals=0),
    )(
        right_side,
        coupling.reshape(brows, bs, kcols),
        child_solution,
        factor_blocks.reshape(brows, bs, bs),
        pattern,
        diag_inverse,
    )


def general(right_side, coupling, child_solution, factor_blocks, pattern, diag_inverse):
    nrow = lax.axis_size("row")
    ncol = lax.axis_size("col")
    row_index = lax.axis_index("row")
    col_index = lax.axis_index("col")
    brows = coupling.shape[0]
    blk_size = coupling.shape[2]
    kcols = coupling.shape[3]
    rhs_count = child_solution.shape[1]
    nblk = pattern.shape[0]
    group = ncol // nblk
    part_rows = blk_size // group
    my_block = col_index // group
    my_offset = col_index % group * part_rows
    flat = coupling.reshape(brows * blk_size, kcols)
    update = jnp.dot(
        flat,
        lax.all_gather(child_solution, "row", axis=0, tiled=True),
        preferred_element_type=jnp.float32,
    )
    update = update.reshape(brows, blk_size, rhs_count)
    rhs_part = right_side.reshape(part_rows, rhs_count)
    placed = lax.dynamic_update_slice(
        jnp.zeros((blk_size, rhs_count), jnp.float32), rhs_part, (my_offset, jnp.int32(0))
    )
    blocks = factor_blocks.reshape(brows, blk_size, part_rows)
    inv_rows = diag_inverse.reshape(part_rows, blk_size)

    def advance(j, solved):
        j_row = j % nrow
        j_arow = j // nrow
        flags = lax.dynamic_index_in_dim(pattern, j, 0, keepdims=False)
        flag = lax.dynamic_index_in_dim(flags, my_block, 0, keepdims=False)
        keep = (flag > 0) & (my_block < j)
        masked = jnp.where(keep, solved, jnp.zeros_like(solved))
        row_blocks = lax.dynamic_index_in_dim(blocks, j_arow, 0, keepdims=False)
        partial_value = jnp.dot(row_blocks, masked, preferred_element_type=jnp.float32)
        partial_value = partial_value + lax.dynamic_index_in_dim(update, j_arow, 0, keepdims=False)
        partial_value = jnp.where(my_block == j, placed, jnp.zeros_like(placed)) - partial_value
        partial_value = jnp.where(row_index == j_row, partial_value, jnp.zeros_like(partial_value))
        total = lax.psum(partial_value, ("col", "row"))
        fresh = jnp.dot(
            inv_rows, total.astype(jnp.bfloat16), preferred_element_type=jnp.float32
        ).astype(jnp.bfloat16)
        return jnp.where(my_block == j, fresh, solved)

    start_state = jnp.zeros((part_rows, rhs_count), jnp.bfloat16)
    solved = lax.fori_loop(0, nblk, advance, start_state)
    return solved.reshape(1, part_rows, rhs_count)


def solution(mesh):
    nrow, ncol = mesh.shape["row"], mesh.shape["col"]
    in_specs = (
        P("col", None, None),
        P(None, "row", None, "col"),
        P(("col", "row"), None),
        P(None, "row", None, "col", None),
        P(),
        P("col", None, None),
    )

    def per_device(right_side, coupling, child_solution, factor_blocks, pattern, diag_inverse):
        paired = nrow == 4 and ncol == 8 and pattern.shape[0] == 8
        body = fused if paired else general
        return body(right_side, coupling, child_solution, factor_blocks, pattern, diag_inverse)

    return jax.shard_map(
        per_device, mesh=mesh, in_specs=in_specs, out_specs=P("col", None, None), check_vma=False
    )
```

time: 74 us -> 64 us (0.86)
  Pallas kernels: 67.8 us -> 62.3 us
  local copies, waits for them, and re-layouts: 5.46 us -> 1.57 us
    pallas_call x1, Pallas kernels: 67.8 us -> 62.3 us  [fused(): pl.pallas_call(functools.partial(kernel, nch), out_shape=jax.ShapeDtypeSt...]
    unnamed x11 -> x1, local copies, waits for them, and re-layouts: 5.46 us -> 1.57 us
where the time goes in v2:
time: 64 us; the launch traced here: 63.9 us
  Pallas kernels  62.3 us (97%)
  local copies, waits for them, and re-layouts  1.57 us (2%)
    pallas_call x1, Pallas kernels, fused(): pl.pallas_call(functools.partial(kernel, nch), out_shape=jax.ShapeDtypeSt...  62.3 us
    unnamed x1, local copies, waits for them, and re-layouts  1.57 us

profile of v2, /device:TPU:25, one launch (start us, length us, event | category | flops | bytes accessed | tf_op | source)
XLA Modules:
  0.0 63.9 jit_solution(6964488469574679135)
XLA Ops:
  0.0 62.3 %shard_map.64 = bf16[1,256,256]{2,1,0:T(8,128)(2,1)} custom-call(f32[1,256,256]{2,1,0:T(8,128)} %rhs_hbm.1, bf16[2,256,10240]{2,1,0:T(8,128)(2,1)} %bitcast.2, bf16[2560,256]{1,0:T(8,128)(2,1)} %child_hbm.1, bf16[2,256,256]{2,1,0:T(8,128)(2,1)} %bitcast.3, s32[8,8]{1,0:T(8,128)} %pat_hbm.1, bf16[1,256,256]{2,1,0:T(8,128)(2,1)} %dinv_hbm.1), custom_call_target="tpu_custom_call" | custom-call | flops 2684354560 | bytes 10485760 | tf_op jit(solution)/shard_map/pallas_call | solution.py:319
  62.3 1.6 %copy.8 = bf16[1,256,256]{2,1,0:T(8,128)(2,1)} copy(bf16[1,256,256]{2,1,0:T(8,128)(2,1)} %shard_map.64) | data formatting | bytes 262144

commit v3 on v2

--- a/solution.py
+++ b/solution.py
@@ -20,7 +20,7 @@
     nch, rhs_hbm, cpl_hbm, child_hbm, fac_hbm, pat_hbm, dinv_hbm, out_ref,
     pat_ref, cpl, gath, acc, fac, xpart, xrecv, part, precv, diag, rside, below, gain, rest, sol,
     loc_sem, m_send, m_recv, y_send, y_recv, f_send, f_recv, fac_send, fac_recv,
-    d_sem, x_sem, p_send, p_recv, ch_send, ch_recv, o_send, o_recv,
+    d_send, d_recv, r_send, r_recv, x_sem, p_send, p_recv, ch_send, ch_recv, o_send, o_recv, g_send,
 ):
     nrow = lax.axis_size("row")
     ncol = lax.axis_size("col")
@@ -36,7 +36,9 @@
     depth = child_hbm.shape[0]
     step = depth // nch
     half = rhs_hbm.shape[2] // 2
-    solver = (core == 0) & (z % 2 == y)
+    home = (core == 0) & (z % 2 == y)
+    solver = (core == 0) & (z >= 1) & (z <= nslab // 2)
+    slab = 2 * (z - 1) + y
     other_cols = pl.ds(pl.multiple_of((1 - x) * half, half), half)
     my_cols = pl.ds(pl.multiple_of(x * half, half), half)
     halves = (other_cols, my_cols)
@@ -48,7 +50,7 @@
         )
 
     def arrival(ref, sem):
-        return remote(ref, ref, d_sem.at[0], sem, mate, c)
+        return remote(ref, ref, d_send.at[0], sem, mate, c)
 
     own = [
         pltpu.make_async_copy(child_hbm.at[:, halves[h]], gath.at[h, r], loc_sem.at[h])
@@ -56,9 +58,7 @@
     ]
     load = pltpu.make_async_copy(cpl_hbm, cpl, loc_sem.at[2])
     flags = pltpu.make_async_copy(pat_hbm, pat_ref, loc_sem.at[3])
-    d_own = pltpu.make_async_copy(dinv_hbm.at[0], diag.at[x], loc_sem.at[4])
-    r_own = pltpu.make_async_copy(rhs_hbm.at[0, :, my_cols], rside.at[x], loc_sem.at[5])
-    for copy in (own[0], own[1], load, flags, d_own, r_own):
+    for copy in (own[0], own[1], load, flags):
         copy.start()
 
     barrier = pltpu.get_barrier_semaphore()
@@ -96,21 +96,44 @@
     def fac_copy(s, xd):
         return remote(
             fac_hbm.at[s], fac.at[core, c], fac_send.at[s, xd], fac_recv.at[core, c],
-            2 * y, 2 * (y + 2 * s) + xd)
+            2 * y, 2 * (1 + s) + xd)
+
+    def fac_self(s, xd):
+        return (core == 0) & (c == 2 * (1 + s) + xd)
 
     for s in range(2):
-        @pl.when(c < r + nrow * s)
-        def _():
-            for xd in range(2):
+        for xd in range(2):
+            @pl.when((c < r + nrow * s) & jnp.logical_not(fac_self(s, xd)))
+            def _():
                 fac_copy(s, xd).start()
 
-    d_copy = remote(dinv_hbm.at[0], diag.at[x], d_sem.at[0], d_sem.at[1], r, beside)
-    r_copy = remote(rhs_hbm.at[0, :, other_cols], rside.at[x], d_sem.at[2], d_sem.at[3], r, beside)
-
-    @pl.when(solver)
-    def _():
-        d_copy.start()
-        r_copy.start()
+            @pl.when((c < r + nrow * s) & fac_self(s, xd))
+            def _():
+                pltpu.make_async_copy(fac_hbm.at[s], fac.at[core, c], fac_recv.at[core, c]).start()
+
+    def d_copy(xd):
+        return remote(
+            dinv_hbm.at[0], diag.at[x], d_send.at[xd], d_recv.at[x], r, 2 * (1 + z // 2) + xd)
+
+    def r_copy(xd):
+        return remote(
+            rhs_hbm.at[0, :, pl.ds(xd * half, half)], rside.at[x], r_send.at[xd], r_recv.at[x],
+            r, 2 * (1 + z // 2) + xd)
+
+    def d_self(xd):
+        return (z == 1 + z // 2) & (x == xd)
+
+    for xd in range(2):
+        @pl.when(home & jnp.logical_not(d_self(xd)))
+        def _():
+            d_copy(xd).start()
+            r_copy(xd).start()
+
+        @pl.when(home & d_self(xd))
+        def _():
+            pltpu.make_async_copy(dinv_hbm.at[0], diag.at[x], d_recv.at[x]).start()
+            pltpu.make_async_copy(
+                rhs_hbm.at[0, :, pl.ds(xd * half, half)], rside.at[x], r_recv.at[x]).start()
 
     acc[...] = jnp.zeros_like(acc)
 
@@ -121,22 +144,21 @@
             acc[h, b] += dot(cpl[b, :, cols], block)
 
     def flag(p, k):
-        return jnp.where(pat_ref[2 * z + p, k] > 0, 1.0, 0.0).astype(F32)
+        return jnp.where(pat_ref[2 * slab + p, k] > 0, 1.0, 0.0).astype(F32)
 
     def prepare():
-        d_own.wait()
-        r_own.wait()
-        arrival(diag.at[1 - x], d_sem.at[1]).wait_recv()
-        arrival(rside.at[1 - x], d_sem.at[3]).wait_recv()
+        for p in range(2):
+            arrival(diag.at[p], d_recv.at[p]).wait_recv()
+            arrival(rside.at[p], r_recv.at[p]).wait_recv()
         for p in range(2):
             for k in range(ncol - 1):
-                @pl.when(k < 2 * z + p)
+                @pl.when(k < 2 * slab + p)
                 def _():
                     arrival(fac.at[p, k], fac_recv.at[p, k]).wait_recv()
-        inner = flag(1, 2 * z) * dot(fac[1, 2 * z], diag[0])
+        inner = flag(1, 2 * slab) * dot(fac[1, 2 * slab], diag[0])
         below[...] = -dot(diag[1], inner.astype(BF16)).astype(BF16)
         for zz in range(nslab - 1):
-            @pl.when(zz < z)
+            @pl.when(zz < slab)
             def _():
                 @pl.loop(0, 2)
                 def _(q):
@@ -191,10 +213,10 @@
     def p_copy(s):
         return remote(
             part.at[s], precv.at[core, z], p_send.at[s], p_recv.at[core, z],
-            2 * y, 2 * (y + 2 * s) + x)
+            2 * y, 2 * (1 + s) + x)
 
     def p_self(s):
-        return solver & (z == y + 2 * s)
+        return solver & (z == 1 + s)
 
     for s in range(2):
         acc[1, s] = acc[1, s] + xrecv[s].astype(F32)
@@ -206,29 +228,26 @@
 
     def chain_copy(zd):
         return remote(
-            sol.at[z], sol.at[z], ch_send.at[zd], ch_recv.at[z], 2 * (zd % 2), 2 * zd + x)
+            sol.at[slab], sol.at[slab], ch_send.at[zd], ch_recv.at[slab],
+            2 * (zd % 2), 2 * (1 + zd // 2) + x)
 
     def out_copy(xo, ro):
         return remote(
-            sol.at[z, xo], out_ref.at[0, :, my_cols], o_send.at[xo, ro], o_recv.at[x], ro, 2 * z + xo)
+            sol.at[slab, xo], out_ref.at[0, :, my_cols], o_send.at[xo, ro], o_recv.at[x],
+            ro, 2 * slab + xo)
 
     def out_self(xo, ro):
-        return (r == ro) & (x == xo)
+        return (r == ro) & (slab == z) & (x == xo)
 
     def send_out(xo):
-        for ro in range(nrow):
+        for ro in range(0, nrow, 2):
             @pl.when(jnp.logical_not(out_self(xo, ro)))
             def _():
                 out_copy(xo, ro).start()
-
-    @pl.when(jnp.logical_not(solver))
-    def _():
-        d_own.wait()
-        r_own.wait()
 
     @pl.when(solver)
     def _():
-        rest[0] = rside[0] - acc[1, z // 2]
+        rest[0] = rside[0] - acc[1, z - 1]
         rest[1] = rside[1]
         for p in range(2):
             for k in range(nslab):
@@ -246,25 +265,41 @@
         rest[0] = dot(diag[0], upper)
         rest[1] = dot(diag[1], lower) + dot(below[...], upper)
         for zz in range(nslab - 1):
-            @pl.when(zz < z)
+            @pl.when(zz < slab)
             def _():
                 arrival(sol.at[zz], ch_recv.at[zz]).wait_recv()
                 for p in range(2):
                     rest[p] = rest[p] - (dot(gain[zz, 0, p], sol[zz, 0]) + dot(gain[zz, 1, p], sol[zz, 1]))
 
-        sol[z] = rest[...].astype(BF16)
+        sol[slab] = rest[...].astype(BF16)
         for zd in range(1, nslab):
-            @pl.when(zd == z + 1)
+            @pl.when(zd == slab + 1)
             def _():
                 chain_copy(zd).start()
                 chain_copy(zd).wait_send()
         for zd in range(2, nslab):
-            @pl.when(zd > z + 1)
+            @pl.when(zd > slab + 1)
             def _():
                 chain_copy(zd).start()
         send_out(0)
         send_out(1)
-        out_ref[0, :, my_cols] = sol[z, x]
+
+        @pl.when(slab == z)
+        def _():
+            out_ref[0, :, my_cols] = sol[slab, x]
+
+    def relay(xs):
+        spot = out_ref.at[0, :, pl.ds(xs * half, half)]
+        return remote(spot, spot, g_send.at[xs], o_recv.at[xs], mate, c)
+
+    for xs in range(2):
+        @pl.when(jnp.logical_not(solver & (slab == z) & (x == xs)))
+        def _():
+            arrival(out_ref.at[0, :, pl.ds(xs * half, half)], o_recv.at[xs]).wait_recv()
+
+        @pl.when(core == 0)
+        def _():
+            relay(xs).start()
 
     m_copy(0).wait_send()
     m_copy(1).wait_send()
@@ -276,30 +311,33 @@
             forward(h, i).wait_send()
 
     for s in range(2):
-        @pl.when(c < r + nrow * s)
-        def _():
-            for xd in range(2):
+        for xd in range(2):
+            @pl.when((c < r + nrow * s) & jnp.logical_not(fac_self(s, xd)))
+            def _():
                 fac_copy(s, xd).wait_send()
 
+            @pl.when((s == 0) & home & jnp.logical_not(d_self(xd)))
+            def _():
+                d_copy(xd).wait_send()
+                r_copy(xd).wait_send()
+
         @pl.when(jnp.logical_not(p_self(s)))
         def _():
             p_copy(s).wait_send()
 
-    for xs in range(2):
-        @pl.when(jnp.logical_not(solver & (x == xs)))
-        def _():
-            arrival(out_ref.at[0, :, pl.ds(xs * half, half)], o_recv.at[xs]).wait_recv()
+    @pl.when(core == 0)
+    def _():
+        for xs in range(2):
+            relay(xs).wait_send()
 
     @pl.when(solver)
     def _():
-        d_copy.wait_send()
-        r_copy.wait_send()
         for zd in range(2, nslab):
-            @pl.when(zd > z + 1)
+            @pl.when(zd > slab + 1)
             def _():
                 chain_copy(zd).wait_send()
         for xo in range(2):
-            for ro in range(nrow):
+            for ro in range(0, nrow, 2):
                 @pl.when(jnp.logical_not(out_self(xo, ro)))
                 def _():
                     out_copy(xo, ro).wait_send()
@@ -337,10 +375,10 @@
             pltpu.VMEM((ncol // 2 - 1, 2, 2, bs, bs), BF16),
             pltpu.VMEM((2, bs, half), F32),
             pltpu.VMEM((ncol // 2, 2, bs, half), BF16),
-            dma((6,)), dma((2,)), dma((2,)),
+            dma((4,)), dma((2,)), dma((2,)),
             dma((2, nch)), dma((2, nch)), dma((2, nch)), dma((2, nch)),
-            dma((2, 2)), dma((2, ncol)), dma((4,)), dma((2,)), dma((2,)), dma((2, ncol // 2)),
-            dma((ncol // 2,)), dma((ncol // 2,)), dma((2, nrow)), dma((2,)),
+            dma((2, 2)), dma((2, ncol)), dma((2,)), dma((2,)), dma((2,)), dma((2,)), dma((2,)), dma((2,)), dma((2, ncol // 2)),
+            dma((ncol // 2,)), dma((ncol // 2,)), dma((2, nrow)), dma((2,)), dma((2,)),
         ],
         compiler_params=pltpu.CompilerParams(
             collective_id=0, has_side_effects=True, vmem_limit_bytes=62 * 1024 * 1024

time: 64 us -> 62.6 us (0.978); the launches traced: 63.9 us -> 61.8 us
  Pallas kernels: 62.3 us -> 60.2 us
    pallas_call x1, Pallas kernels: 62.3 us -> 60.2 us  [fused(): pl.pallas_call(functools.partial(kernel, nch), out_shape=jax.ShapeDtypeSt...]
where the time goes in v3:
time: 62.6 us; the launch traced here: 61.8 us
  Pallas kernels  60.2 us (96%)
  local copies, waits for them, and re-layouts  1.57 us (3%)
    pallas_call x1, Pallas kernels, fused(): pl.pallas_call(functools.partial(kernel, nch), out_shape=jax.ShapeDtypeSt...  60.2 us
    unnamed x1, local copies, waits for them, and re-layouts  1.57 us

profile of v3, /device:TPU:25, one launch (start us, length us, event | category | flops | bytes accessed | tf_op | source)
XLA Modules:
  0.0 61.8 jit_solution(2635369974998918110)
XLA Ops:
  0.0 60.2 %shard_map.64 = bf16[1,256,256]{2,1,0:T(8,128)(2,1)} custom-call(f32[1,256,256]{2,1,0:T(8,128)} %rhs_hbm.1, bf16[2,256,10240]{2,1,0:T(8,128)(2,1)} %bitcast.2, bf16[2560,256]{1,0:T(8,128)(2,1)} %child_hbm.1, bf16[2,256,256]{2,1,0:T(8,128)(2,1)} %bitcast.3, s32[8,8]{1,0:T(8,128)} %pat_hbm.1, bf16[1,256,256]{2,1,0:T(8,128)(2,1)} %dinv_hbm.1), custom_call_target="tpu_custom_call" | custom-call | flops 2684354560 | bytes 10485760 | tf_op jit(solution)/shard_map/pallas_call | solution.py:357
  60.2 1.6 %copy.8 = bf16[1,256,256]{2,1,0:T(8,128)(2,1)} copy(bf16[1,256,256]{2,1,0:T(8,128)(2,1)} %shard_map.64) | data formatting | bytes 262144
